TPU v7x, 128 devices: a whole 4x4x4 slice. The times are simulated.
128 devices in a mesh: slab: 32 (over z, y, core), col: 4 (over x).
Axes of the slice: x: 4, y: 4, z: 4, core: 2. Of those that a mesh axis runs over, the one named last changes fastest.
Arguments:
- cell_rhs: float32 [3, 128, 64, 8, 256], P(None, None, 'slab', 'col'), may hold values from -6 to 6
- well_rhs: float32 [256, 3, 128], P(('slab', 'col')), may hold values from -6 to 6
- cell_colors: int32 [64, 8, 256], P('slab', 'col'), may hold values from 0 to 3, as said below
- incoming: float32 [6, 3, 3, 64, 8, 256], P(None, None, None, 'slab', 'col'), may hold values from -1.2 to 1.2
- pivot_inv: float32 [3, 3, 64, 8, 256], P(None, None, 'slab', 'col'), may hold values from -1 to 2
- perf_cell: int32 [8192], P(('slab', 'col')), may hold values from 0 to 1023
- perf_well: int32 [8192], P(('slab', 'col')), may hold values from 0 to 255
- perf_out: float32 [8192, 3, 3], P(('slab', 'col')), may hold values from -0.6 to 0.6
- perf_in: float32 [8192, 3, 3], P(('slab', 'col')), may hold values from -1.2 to 1.2
- well_pivot_inv: float32 [256, 3, 3], P(('slab', 'col')), may hold values from -1 to 2
Outputs:
- cell_adjoint: float32 [3, 128, 64, 8, 256], P(None, None, 'slab', 'col')
- well_adjoint: float32 [256, 3, 128], P(('slab', 'col'))
Inputs may be any that keep to these rules, and one draw needn't show every extreme that they name: `cell_colors`: the parity of a cell's color equals the parity of its x + y + z. `perf_cell`: index of the cell within the 2 x 2 x 256 block of the device that holds the perforation. `perf_well`: well w is owned by the device holding entry w of the well arrays.
All inputs are finite; a program needn't handle non-finite values.
Results may differ from a plain program's by a relative error of at most 0.00011.
Values sent between devices are 32-bit elements; how exact they have to be, the bound alone decides.
No kernel may reach another device: no remote copies, remote signals or barrier semaphores. Data moves between devices by JAX's collectives and lax.ppermute only.
A program may use at most 128 MiB of HBM per device.

v0:
```python
import jax
import jax.numpy as jnp
from jax import lax
from jax.sharding import PartitionSpec as P


def with_halo(cells, sides, width):
    for axis, dim in sides:
        count = lax.axis_size(axis)
        ends = count - 1
        head = lax.slice_in_dim(cells, 0, width, axis=dim)
        tail = lax.slice_in_dim(cells, cells.shape[dim] - width, cells.shape[dim], axis=dim)
        cells = jnp.concatenate(
            [
                lax.ppermute(tail, axis, [(i, (i + 1) % count) for i in range(ends)]),
                cells,
                lax.ppermute(head, axis, [((i + 1) % count, i) for i in range(ends)]),
            ],
            axis=dim,
        )
    return cells


def apply_blocks(blocks, vector):
    return (
        blocks[0][:, None] * vector[0][None]
        + blocks[1][:, None] * vector[1][None]
        + blocks[2][:, None] * vector[2][None]
    )


def well_apply(blocks, vector):
    return (
        blocks[:, 0, :, None] * vector[:, 0, None, :]
        + blocks[:, 1, :, None] * vector[:, 1, None, :]
        + blocks[:, 2, :, None] * vector[:, 2, None, :]
    )


def z_lower(values):
    widths = [(0, 0)] * (values.ndim - 1) + [(1, 0)]
    return jnp.pad(values, widths)[..., :-1]


def z_upper(values):
    widths = [(0, 0)] * (values.ndim - 1) + [(0, 1)]
    return jnp.pad(values, widths)[..., 1:]


def face_sum(incoming, padded):
    size_x = padded.shape[2] - 2
    size_y = padded.shape[3] - 2
    center = padded[:, :, 1 : size_x + 1, 1 : size_y + 1]
    summed = apply_blocks(incoming[0], padded[:, :, 0:size_x, 1 : size_y + 1])
    summed = summed + apply_blocks(incoming[1], padded[:, :, 2 : size_x + 2, 1 : size_y + 1])
    summed = summed + apply_blocks(incoming[2], padded[:, :, 1 : size_x + 1, 0:size_y])
    summed = summed + apply_blocks(incoming[3], padded[:, :, 1 : size_x + 1, 2 : size_y + 2])
    summed = summed + apply_blocks(incoming[4], z_lower(center))
    summed = summed + apply_blocks(incoming[5], z_upper(center))
    return summed


def neighbours(incoming, values):
    padded = with_halo(values, (("slab", 2), ("col", 3)), 1)
    summed = face_sum(incoming, padded)
    return summed


def per_device(
    cell_rhs,
    well_rhs,
    cell_colors,
    incoming,
    pivot_inv,
    perf_cell,
    perf_well,
    perf_out,
    perf_in,
    well_pivot_inv,
):
    forward = jnp.zeros_like(cell_rhs)
    for color_index in range(4):
        if color_index == 0:
            source = cell_rhs
        else:
            source = cell_rhs - neighbours(incoming, forward)
        forward = jnp.where(
            (cell_colors == color_index)[None, None], apply_blocks(pivot_inv, source), forward
        )
    rhs_count = cell_rhs.shape[1]
    cell_count = cell_rhs.shape[2] * cell_rhs.shape[3] * cell_rhs.shape[4]
    perf_count = perf_cell.shape[0]
    own_count = well_pivot_inv.shape[0]
    well_count = lax.axis_size(("slab", "col")) * own_count
    flat_cells = forward.reshape(3 * rhs_count, cell_count)
    cell_hot = (
        lax.broadcasted_iota(jnp.int32, (cell_count, perf_count), 0) == perf_cell[None, :]
    ).astype(jnp.float32)
    at_perfs = lax.dot_general(
        flat_cells, cell_hot, (((1,), (0,)), ((), ())), precision=lax.Precision.HIGHEST
    )
    at_perfs = jnp.transpose(at_perfs.reshape(3, rhs_count, perf_count), (2, 0, 1))
    partial_value = well_apply(perf_out, at_perfs)
    well_hot = (
        lax.broadcasted_iota(jnp.int32, (well_count, perf_count), 0) == perf_well[None, :]
    ).astype(jnp.float32)
    summed_wells = jnp.dot(
        well_hot, partial_value.reshape(perf_count, 3 * rhs_count), precision=lax.Precision.HIGHEST
    ).reshape(well_count, 3, rhs_count)
    own_sum = lax.psum_scatter(summed_wells, ("slab", "col"), scatter_dimension=0, tiled=True)
    well_adjoint = well_apply(well_pivot_inv, well_rhs - own_sum)
    adjoint_all = lax.all_gather(well_adjoint, ("slab", "col"), axis=0, tiled=True)
    well_at_perfs = lax.dot_general(
        well_hot,
        adjoint_all.reshape(well_count, 3 * rhs_count),
        (((0,), (0,)), ((), ())),
        precision=lax.Precision.HIGHEST,
    )
    perf_fixes = well_apply(perf_in, well_at_perfs.reshape(perf_count, 3, rhs_count))
    cell_fix = lax.dot_general(
        perf_fixes.reshape(perf_count, 3 * rhs_count),
        cell_hot,
        (((0,), (1,)), ((), ())),
        precision=lax.Precision.HIGHEST,
    )
    corrected = forward - cell_fix.reshape(forward.shape)
    backward = jnp.zeros_like(corrected)
    for color_index in (3, 2, 1, 0):
        if color_index == 3:
            source = corrected
        else:
            source = corrected - neighbours(incoming, backward)
        backward = jnp.where((cell_colors == color_index)[None, None], source, backward)
    return (backward, well_adjoint)


def solution(mesh):
    placed = (
        P(None, None, "slab", "col", None),
        P(("slab", "col"), None, None),
        P("slab", "col", None),
        P(None, None, None, "slab", "col", None),
        P(None, None, "slab", "col", None),
        P(("slab", "col")),
        P(("slab", "col")),
        P(("slab", "col"), None, None),
        P(("slab", "col"), None, None),
        P(("slab", "col"), None, None),
    )
    return jax.shard_map(
        per_device,
        mesh=mesh,
        in_specs=placed,
        out_specs=(P(None, None, "slab", "col", None), P(("slab", "col"), None, None)),
        check_vma=False,
    )
```

profile of v0, /device:TPU:38, one launch (start us, length us, event | category | flops | bytes accessed | tf_op | source)
XLA Modules:
  0.0 628.5 jit_solution(2131001356934884733)
XLA Ops:
  14.3 5.8 collective-permute-start.1
  20.1 7.7 %collective-permute-done = f32[3,128,1,2,256]{4,1,3,2,0:T(8,128)S(1)} collective-permute-done((f32[3,128,1,2,256]{4,1,3,2,0:T(8,128)S(1)}, f32[3,128,1,2,256]{4,1,3,2,0:T(8,128)S(1)}, u32[]{:S(2)}, u32[]{:S(2)}) %collective-permute-start) | collective-permute-done | bytes 786464 | tf_op jit(solution)/shard_map/ppermute | solution.py:15
  35.3 31.2 %collective-permute-done.3 = f32[3,128,4,1,256]{4,1,3,2,0:T(8,128)S(1)} collective-permute-done((f32[3,128,4,1,256]{4,1,3,2,0:T(8,128)S(1)}, f32[3,128,4,1,256]{4,1,3,2,0:T(8,128)S(1)}, u32[]{:S(2)}, u32[]{:S(2)}) %collective-permute-start.3) | collective-permute-done | bytes 1572896 | tf_op jit(solution)/shard_map/ppermute | solution.py:17
  66.9 3.9 collective-permute-done.2
  71.3 3.2 add_subtract_fusion.2
  78.5 5.8 collective-permute-start.5
  84.2 7.7 %collective-permute-done.4 = f32[3,128,1,2,256]{4,1,3,2,0:T(8,128)S(1)} collective-permute-done((f32[3,128,1,2,256]{4,1,3,2,0:T(8,128)S(1)}, f32[3,128,1,2,256]{4,1,3,2,0:T(8,128)S(1)}, u32[]{:S(2)}, u32[]{:S(2)}) %collective-permute-start.4) | collective-permute-done | bytes 786464 | tf_op jit(solution)/shard_map/ppermute | solution.py:15
  99.2 29.9 %collective-permute-done.7 = f32[3,128,4,1,256]{4,1,3,2,0:T(8,128)S(1)} collective-permute-done((f32[3,128,4,1,256]{4,1,3,2,0:T(8,128)S(1)}, f32[3,128,4,1,256]{4,1,3,2,0:T(8,128)S(1)}, u32[]{:S(2)}, u32[]{:S(2)}) %collective-permute-start.7) | collective-permute-done | bytes 1572896 | tf_op jit(solution)/shard_map/ppermute | solution.py:17
  129.6 3.7 collective-permute-done.6
  133.8 3.2 add_subtract_fusion.1
  141.3 5.8 collective-permute-start.9
  147.0 7.7 %collective-permute-done.8 = f32[3,128,1,2,256]{4,1,3,2,0:T(8,128)S(1)} collective-permute-done((f32[3,128,1,2,256]{4,1,3,2,0:T(8,128)S(1)}, f32[3,128,1,2,256]{4,1,3,2,0:T(8,128)S(1)}, u32[]{:S(2)}, u32[]{:S(2)}) %collective-permute-start.8) | collective-permute-done | bytes 786464 | tf_op jit(solution)/shard_map/ppermute | solution.py:15
  159.3 3.5 collective-permute-start.11
  204.1 3.2 add_subtract_fusion
  220.9 5.3 fusion
  227.8 147.1 %all-reduce.15.cloned.1.call-done = f32[256,3,128]{2,0,1:T(8,128)} async-done(((f32[256,3,128]{2,0,1:T(8,128)}), f32[256,3,128]{2,0,1:T(8,128)}) %all-reduce.15.cloned.1.call-update) | async-done | bytes 393232
  376.3 52.6 %all_gather.3 = f32[256,3,128]{2,1,0:T(4,128)} all-gather(f32[2,3,128]{2,1,0:T(4,128)S(1)} %multiply_add_fusion.3), channel_id=1, replica_groups=mesh['slab'=32,'col'=4] {'slab','col'}, dimensions={0}, use_global_device_ids=true | all-gather | bytes 396288 | tf_op jit(solution)/shard_map/all_gather | solution.py:112
  436.8 5.2 collective-permute-start.13
  442.0 7.7 %collective-permute-done.12 = f32[3,128,1,2,256]{4,1,3,2,0:T(8,128)S(1)} collective-permute-done((f32[3,128,1,2,256]{4,1,3,2,0:T(8,128)S(1)}, f32[3,128,1,2,256]{4,1,3,2,0:T(8,128)S(1)}, u32[]{:S(2)}, u32[]{:S(2)}) %collective-permute-start.12) | collective-permute-done | bytes 786464 | tf_op jit(solution)/shard_map/ppermute | solution.py:15
  452.0 3.4 collective-permute-start.15
  457.3 30.2 %collective-permute-done.15 = f32[3,128,4,1,256]{4,1,3,2,0:T(8,128)S(1)} collective-permute-done((f32[3,128,4,1,256]{4,1,3,2,0:T(8,128)S(1)}, f32[3,128,4,1,256]{4,1,3,2,0:T(8,128)S(1)}, u32[]{:S(2)}, u32[]{:S(2)}) %collective-permute-start.15) | collective-permute-done | bytes 1572896 | tf_op jit(solution)/shard_map/ppermute | solution.py:17
  488.1 3.6 collective-permute-done.14
  497.7 5.8 collective-permute-start.17
  503.4 7.7 %collective-permute-done.16 = f32[3,128,1,2,256]{4,1,3,2,0:T(8,128)S(1)} collective-permute-done((f32[3,128,1,2,256]{4,1,3,2,0:T(8,128)S(1)}, f32[3,128,1,2,256]{4,1,3,2,0:T(8,128)S(1)}, u32[]{:S(2)}, u32[]{:S(2)}) %collective-permute-start.16) | collective-permute-done | bytes 786464 | tf_op jit(solution)/shard_map/ppermute | solution.py:15
  518.5 29.6 %collective-permute-done.19 = f32[3,128,4,1,256]{4,1,3,2,0:T(8,128)S(1)} collective-permute-done((f32[3,128,4,1,256]{4,1,3,2,0:T(8,128)S(1)}, f32[3,128,4,1,256]{4,1,3,2,0:T(8,128)S(1)}, u32[]{:S(2)}, u32[]{:S(2)}) %collective-permute-start.19) | collective-permute-done | bytes 1572896 | tf_op jit(solution)/shard_map/ppermute | solution.py:17
  548.6 3.7 collective-permute-done.18
  552.9 5.7 subtract_select_fusion.1
  560.6 5.8 collective-permute-start.21
  566.3 7.7 %collective-permute-done.20 = f32[3,128,1,2,256]{4,1,3,2,0:T(8,128)S(1)} collective-permute-done((f32[3,128,1,2,256]{4,1,3,2,0:T(8,128)S(1)}, f32[3,128,1,2,256]{4,1,3,2,0:T(8,128)S(1)}, u32[]{:S(2)}, u32[]{:S(2)}) %collective-permute-start.20) | collective-permute-done | bytes 786464 | tf_op jit(solution)/shard_map/ppermute | solution.py:15
  576.4 3.6 collective-permute-start.23
  582.5 28.4 %collective-permute-done.23 = f32[3,128,4,1,256]{4,1,3,2,0:T(8,128)S(1)} collective-permute-done((f32[3,128,4,1,256]{4,1,3,2,0:T(8,128)S(1)}, f32[3,128,4,1,256]{4,1,3,2,0:T(8,128)S(1)}, u32[]{:S(2)}, u32[]{:S(2)}) %collective-permute-start.23) | collective-permute-done | bytes 1572896 | tf_op jit(solution)/shard_map/ppermute | solution.py:17
  611.4 3.8 collective-permute-done.22
  (245 shorter events, 133.4 us)
Async XLA Ops:
  7.2 367.7 %all-reduce.15.cloned.1.call-start = ((), (), s32[]{:S(2)}) async-start(), calls=%async_computation | async-start | bytes 786432
  12.4 15.4 %collective-permute-start = (f32[3,128,1,2,256]{4,1,3,2,0:T(8,128)S(1)}, f32[3,128,1,2,256]{4,1,3,2,0:T(8,128)S(1)}, u32[]{:S(2)}, u32[]{:S(2)}) collective-permute-start(f32[3,128,1,2,256]{4,1,3,2,0:T(8,128)S(1)} %get-tuple-element.158), channel_id=1, source_target_pairs={{0,4},{4,8},{8,12},{12,16},{16,20},{20,24},{24,28},{28,32},{32,36}... | collective-permute-start | bytes 2359304 | tf_op jit(solution)/shard_map/ppermute | solution.py:15
  14.3 15.2 %collective-permute-start.1 = (f32[3,128,1,2,256]{4,1,3,2,0:T(8,128)S(1)}, f32[3,128,1,2,256]{4,1,3,2,0:T(8,128)S(1)}, u32[]{:S(2)}, u32[]{:S(2)}) collective-permute-start(f32[3,128,1,2,256]{4,1,3,2,0:T(8,128)S(1)} %get-tuple-element.159), channel_id=1, source_target_pairs={{4,0},{8,4},{12,8},{16,12},{20,16},{24,20},{28,24},{32,28},{36,32}... | collective-permute-start | bytes 2359304 | tf_op jit(solution)/shard_map/ppermute | solution.py:17
  30.2 36.3 %collective-permute-start.3 = (f32[3,128,4,1,256]{4,1,3,2,0:T(8,128)S(1)}, f32[3,128,4,1,256]{4,1,3,2,0:T(8,128)S(1)}, u32[]{:S(2)}, u32[]{:S(2)}) collective-permute-start(f32[3,128,4,1,256]{4,1,3,2,0:T(8,128)S(1)} %get-tuple-element.55), channel_id=1, source_target_pairs={{1,0},{2,1},{3,2},{5,4},{6,5},{7,6},{9,8},{10,9},{11,10},{13,12},{... | collective-permute-start | bytes 4718600 | tf_op jit(solution)/shard_map/ppermute | solution.py:17
  33.0 37.8 %collective-permute-start.2 = (f32[3,128,4,1,256]{4,1,3,2,0:T(8,128)S(1)}, f32[3,128,4,1,256]{4,1,3,2,0:T(8,128)S(1)}, u32[]{:S(2)}, u32[]{:S(2)}) collective-permute-start(f32[3,128,4,1,256]{4,1,3,2,0:T(8,128)S(1)} %get-tuple-element.54), channel_id=1, source_target_pairs={{0,1},{1,2},{2,3},{4,5},{5,6},{6,7},{8,9},{9,10},{10,11},{12,13},{... | collective-permute-start | bytes 4718600 | tf_op jit(solution)/shard_map/ppermute | solution.py:15
  35.1 168.9 %copy-start.5 = (f32[3,2,2,256]{3,2,1,0:T(2,128)}, f32[3,2,2,256]{3,2,1,0:T(2,128)S(1)}, u32[]{:S(2)}) copy-start(f32[3,2,2,256]{3,2,1,0:T(2,128)S(1)} %get-tuple-element.165) | copy-start | bytes 36868
  35.1 168.9 %copy-start.7 = (f32[3,2,2,256]{3,2,1,0:T(2,128)}, f32[3,2,2,256]{3,2,1,0:T(2,128)S(1)}, u32[]{:S(2)}) copy-start(f32[3,2,2,256]{3,2,1,0:T(2,128)S(1)} %get-tuple-element.166) | copy-start | bytes 36868
  35.1 168.9 %copy-start.9 = (f32[3,2,2,256]{3,2,1,0:T(2,128)}, f32[3,2,2,256]{3,2,1,0:T(2,128)S(1)}, u32[]{:S(2)}) copy-start(f32[3,2,2,256]{3,2,1,0:T(2,128)S(1)} %get-tuple-element.167) | copy-start | bytes 36868
  35.1 168.9 %copy-start.11 = (f32[3,2,2,256]{3,2,1,0:T(2,128)}, f32[3,2,2,256]{3,2,1,0:T(2,128)S(1)}, u32[]{:S(2)}) copy-start(f32[3,2,2,256]{3,2,1,0:T(2,128)S(1)} %get-tuple-element.168) | copy-start | bytes 36868
  35.1 168.9 %copy-start.13 = (f32[3,2,2,256]{3,2,1,0:T(2,128)}, f32[3,2,2,256]{3,2,1,0:T(2,128)S(1)}, u32[]{:S(2)}) copy-start(f32[3,2,2,256]{3,2,1,0:T(2,128)S(1)} %get-tuple-element.169) | copy-start | bytes 36868
  35.1 168.9 %copy-start.15 = (f32[3,2,2,256]{3,2,1,0:T(2,128)}, f32[3,2,2,256]{3,2,1,0:T(2,128)S(1)}, u32[]{:S(2)}) copy-start(f32[3,2,2,256]{3,2,1,0:T(2,128)S(1)} %get-tuple-element.170) | copy-start | bytes 36868
  35.1 168.9 %copy-start.17 = (f32[3,2,2,256]{3,2,1,0:T(2,128)}, f32[3,2,2,256]{3,2,1,0:T(2,128)S(1)}, u32[]{:S(2)}) copy-start(f32[3,2,2,256]{3,2,1,0:T(2,128)S(1)} %get-tuple-element.171) | copy-start | bytes 36868
  76.6 15.4 %collective-permute-start.4 = (f32[3,128,1,2,256]{4,1,3,2,0:T(8,128)S(1)}, f32[3,128,1,2,256]{4,1,3,2,0:T(8,128)S(1)}, u32[]{:S(2)}, u32[]{:S(2)}) collective-permute-start(f32[3,128,1,2,256]{4,1,3,2,0:T(8,128)S(1)} %get-tuple-element.152), channel_id=1, source_target_pairs={{0,4},{4,8},{8,12},{12,16},{16,20},{20,24},{24,28},{28,32},{32,36}... | collective-permute-start | bytes 2359304 | tf_op jit(solution)/shard_map/ppermute | solution.py:15
  78.5 15.2 %collective-permute-start.5 = (f32[3,128,1,2,256]{4,1,3,2,0:T(8,128)S(1)}, f32[3,128,1,2,256]{4,1,3,2,0:T(8,128)S(1)}, u32[]{:S(2)}, u32[]{:S(2)}) collective-permute-start(f32[3,128,1,2,256]{4,1,3,2,0:T(8,128)S(1)} %get-tuple-element.153), channel_id=1, source_target_pairs={{4,0},{8,4},{12,8},{16,12},{20,16},{24,20},{28,24},{32,28},{36,32}... | collective-permute-start | bytes 2359304 | tf_op jit(solution)/shard_map/ppermute | solution.py:17
  94.3 34.7 %collective-permute-start.7 = (f32[3,128,4,1,256]{4,1,3,2,0:T(8,128)S(1)}, f32[3,128,4,1,256]{4,1,3,2,0:T(8,128)S(1)}, u32[]{:S(2)}, u32[]{:S(2)}) collective-permute-start(f32[3,128,4,1,256]{4,1,3,2,0:T(8,128)S(1)} %get-tuple-element.53), channel_id=1, source_target_pairs={{1,0},{2,1},{3,2},{5,4},{6,5},{7,6},{9,8},{10,9},{11,10},{13,12},{... | collective-permute-start | bytes 4718600 | tf_op jit(solution)/shard_map/ppermute | solution.py:17
  96.8 36.5 %collective-permute-start.6 = (f32[3,128,4,1,256]{4,1,3,2,0:T(8,128)S(1)}, f32[3,128,4,1,256]{4,1,3,2,0:T(8,128)S(1)}, u32[]{:S(2)}, u32[]{:S(2)}) collective-permute-start(f32[3,128,4,1,256]{4,1,3,2,0:T(8,128)S(1)} %get-tuple-element.52), channel_id=1, source_target_pairs={{0,1},{1,2},{2,3},{4,5},{5,6},{6,7},{8,9},{9,10},{10,11},{12,13},{... | collective-permute-start | bytes 4718600 | tf_op jit(solution)/shard_map/ppermute | solution.py:15
  139.4 15.4 %collective-permute-start.8 = (f32[3,128,1,2,256]{4,1,3,2,0:T(8,128)S(1)}, f32[3,128,1,2,256]{4,1,3,2,0:T(8,128)S(1)}, u32[]{:S(2)}, u32[]{:S(2)}) collective-permute-start(f32[3,128,1,2,256]{4,1,3,2,0:T(8,128)S(1)} %get-tuple-element.146), channel_id=1, source_target_pairs={{0,4},{4,8},{8,12},{12,16},{16,20},{20,24},{24,28},{28,32},{32,36}... | collective-permute-start | bytes 2359304 | tf_op jit(solution)/shard_map/ppermute | solution.py:15
  141.3 15.2 %collective-permute-start.9 = (f32[3,128,1,2,256]{4,1,3,2,0:T(8,128)S(1)}, f32[3,128,1,2,256]{4,1,3,2,0:T(8,128)S(1)}, u32[]{:S(2)}, u32[]{:S(2)}) collective-permute-start(f32[3,128,1,2,256]{4,1,3,2,0:T(8,128)S(1)} %get-tuple-element.147), channel_id=1, source_target_pairs={{4,0},{8,4},{12,8},{16,12},{20,16},{24,20},{28,24},{32,28},{36,32}... | collective-permute-start | bytes 2359304 | tf_op jit(solution)/shard_map/ppermute | solution.py:17
  159.3 40.6 %collective-permute-start.11 = (f32[3,128,4,1,256]{4,1,3,2,0:T(8,128)}, f32[3,128,4,1,256]{4,1,3,2,0:T(8,128)}, u32[]{:S(2)}, u32[]{:S(2)}) collective-permute-start(f32[3,128,4,1,256]{4,1,3,2,0:T(8,128)} %get-tuple-element.51), channel_id=1, source_target_pairs={{1,0},{2,1},{3,2},{5,4},{6,5},{7,6},{9,8},{10,9},{11,10},{13,12},{... | collective-permute-start | bytes 4718600 | tf_op jit(solution)/shard_map/ppermute | solution.py:17
  162.9 39.5 %collective-permute-start.10 = (f32[3,128,4,1,256]{4,1,3,2,0:T(8,128)}, f32[3,128,4,1,256]{4,1,3,2,0:T(8,128)}, u32[]{:S(2)}, u32[]{:S(2)}) collective-permute-start(f32[3,128,4,1,256]{4,1,3,2,0:T(8,128)} %get-tuple-element.50), channel_id=1, source_target_pairs={{0,1},{1,2},{2,3},{4,5},{5,6},{6,7},{8,9},{9,10},{10,11},{12,13},{... | collective-permute-start | bytes 4718600 | tf_op jit(solution)/shard_map/ppermute | solution.py:15
  434.3 15.4 %collective-permute-start.12 = (f32[3,128,1,2,256]{4,1,3,2,0:T(8,128)S(1)}, f32[3,128,1,2,256]{4,1,3,2,0:T(8,128)S(1)}, u32[]{:S(2)}, u32[]{:S(2)}) collective-permute-start(f32[3,128,1,2,256]{4,1,3,2,0:T(8,128)S(1)} %get-tuple-element.116), channel_id=1, source_target_pairs={{0,4},{4,8},{8,12},{12,16},{16,20},{20,24},{24,28},{28,32},{32,36}... | collective-permute-start | bytes 2359304 | tf_op jit(solution)/shard_map/ppermute | solution.py:15
  436.8 14.7 %collective-permute-start.13 = (f32[3,128,1,2,256]{4,1,3,2,0:T(8,128)S(1)}, f32[3,128,1,2,256]{4,1,3,2,0:T(8,128)S(1)}, u32[]{:S(2)}, u32[]{:S(2)}) collective-permute-start(f32[3,128,1,2,256]{4,1,3,2,0:T(8,128)S(1)} %get-tuple-element.117), channel_id=1, source_target_pairs={{4,0},{8,4},{12,8},{16,12},{20,16},{24,20},{28,24},{32,28},{36,32}... | collective-permute-start | bytes 2359304 | tf_op jit(solution)/shard_map/ppermute | solution.py:17
  452.0 35.4 %collective-permute-start.15 = (f32[3,128,4,1,256]{4,1,3,2,0:T(8,128)S(1)}, f32[3,128,4,1,256]{4,1,3,2,0:T(8,128)S(1)}, u32[]{:S(2)}, u32[]{:S(2)}) collective-permute-start(f32[3,128,4,1,256]{4,1,3,2,0:T(8,128)S(1)} %get-tuple-element.49), channel_id=1, source_target_pairs={{1,0},{2,1},{3,2},{5,4},{6,5},{7,6},{9,8},{10,9},{11,10},{13,12},{... | collective-permute-start | bytes 4718600 | tf_op jit(solution)/shard_map/ppermute | solution.py:17
  455.4 36.3 %collective-permute-start.14 = (f32[3,128,4,1,256]{4,1,3,2,0:T(8,128)S(1)}, f32[3,128,4,1,256]{4,1,3,2,0:T(8,128)S(1)}, u32[]{:S(2)}, u32[]{:S(2)}) collective-permute-start(f32[3,128,4,1,256]{4,1,3,2,0:T(8,128)S(1)} %get-tuple-element.48), channel_id=1, source_target_pairs={{0,1},{1,2},{2,3},{4,5},{5,6},{6,7},{8,9},{9,10},{10,11},{12,13},{... | collective-permute-start | bytes 4718600 | tf_op jit(solution)/shard_map/ppermute | solution.py:15
  495.7 15.4 %collective-permute-start.16 = (f32[3,128,1,2,256]{4,1,3,2,0:T(8,128)S(1)}, f32[3,128,1,2,256]{4,1,3,2,0:T(8,128)S(1)}, u32[]{:S(2)}, u32[]{:S(2)}) collective-permute-start(f32[3,128,1,2,256]{4,1,3,2,0:T(8,128)S(1)} %get-tuple-element.110), channel_id=1, source_target_pairs={{0,4},{4,8},{8,12},{12,16},{16,20},{20,24},{24,28},{28,32},{32,36}... | collective-permute-start | bytes 2359304 | tf_op jit(solution)/shard_map/ppermute | solution.py:15
  497.7 15.2 %collective-permute-start.17 = (f32[3,128,1,2,256]{4,1,3,2,0:T(8,128)S(1)}, f32[3,128,1,2,256]{4,1,3,2,0:T(8,128)S(1)}, u32[]{:S(2)}, u32[]{:S(2)}) collective-permute-start(f32[3,128,1,2,256]{4,1,3,2,0:T(8,128)S(1)} %get-tuple-element.111), channel_id=1, source_target_pairs={{4,0},{8,4},{12,8},{16,12},{20,16},{24,20},{28,24},{32,28},{36,32}... | collective-permute-start | bytes 2359304 | tf_op jit(solution)/shard_map/ppermute | solution.py:17
  513.5 34.6 %collective-permute-start.19 = (f32[3,128,4,1,256]{4,1,3,2,0:T(8,128)S(1)}, f32[3,128,4,1,256]{4,1,3,2,0:T(8,128)S(1)}, u32[]{:S(2)}, u32[]{:S(2)}) collective-permute-start(f32[3,128,4,1,256]{4,1,3,2,0:T(8,128)S(1)} %get-tuple-element.47), channel_id=1, source_target_pairs={{1,0},{2,1},{3,2},{5,4},{6,5},{7,6},{9,8},{10,9},{11,10},{13,12},{... | collective-permute-start | bytes 4718600 | tf_op jit(solution)/shard_map/ppermute | solution.py:17
  516.3 36.0 %collective-permute-start.18 = (f32[3,128,4,1,256]{4,1,3,2,0:T(8,128)S(1)}, f32[3,128,4,1,256]{4,1,3,2,0:T(8,128)S(1)}, u32[]{:S(2)}, u32[]{:S(2)}) collective-permute-start(f32[3,128,4,1,256]{4,1,3,2,0:T(8,128)S(1)} %get-tuple-element.46), channel_id=1, source_target_pairs={{0,1},{1,2},{2,3},{4,5},{5,6},{6,7},{8,9},{9,10},{10,11},{12,13},{... | collective-permute-start | bytes 4718600 | tf_op jit(solution)/shard_map/ppermute | solution.py:15
  558.6 15.4 %collective-permute-start.20 = (f32[3,128,1,2,256]{4,1,3,2,0:T(8,128)S(1)}, f32[3,128,1,2,256]{4,1,3,2,0:T(8,128)S(1)}, u32[]{:S(2)}, u32[]{:S(2)}) collective-permute-start(f32[3,128,1,2,256]{4,1,3,2,0:T(8,128)S(1)} %get-tuple-element.104), channel_id=1, source_target_pairs={{0,4},{4,8},{8,12},{12,16},{16,20},{20,24},{24,28},{28,32},{32,36}... | collective-permute-start | bytes 2359304 | tf_op jit(solution)/shard_map/ppermute | solution.py:15
  560.6 15.2 %collective-permute-start.21 = (f32[3,128,1,2,256]{4,1,3,2,0:T(8,128)S(1)}, f32[3,128,1,2,256]{4,1,3,2,0:T(8,128)S(1)}, u32[]{:S(2)}, u32[]{:S(2)}) collective-permute-start(f32[3,128,1,2,256]{4,1,3,2,0:T(8,128)S(1)} %get-tuple-element.105), channel_id=1, source_target_pairs={{4,0},{8,4},{12,8},{16,12},{20,16},{24,20},{28,24},{32,28},{36,32}... | collective-permute-start | bytes 2359304 | tf_op jit(solution)/shard_map/ppermute | solution.py:17
  576.4 34.6 %collective-permute-start.23 = (f32[3,128,4,1,256]{4,1,3,2,0:T(8,128)S(1)}, f32[3,128,4,1,256]{4,1,3,2,0:T(8,128)S(1)}, u32[]{:S(2)}, u32[]{:S(2)}) collective-permute-start(f32[3,128,4,1,256]{4,1,3,2,0:T(8,128)S(1)} %get-tuple-element.45), channel_id=1, source_target_pairs={{1,0},{2,1},{3,2},{5,4},{6,5},{7,6},{9,8},{10,9},{11,10},{13,12},{... | collective-permute-start | bytes 4718600 | tf_op jit(solution)/shard_map/ppermute | solution.py:17
  580.0 35.1 %collective-permute-start.22 = (f32[3,128,4,1,256]{4,1,3,2,0:T(8,128)S(1)}, f32[3,128,4,1,256]{4,1,3,2,0:T(8,128)S(1)}, u32[]{:S(2)}, u32[]{:S(2)}) collective-permute-start(f32[3,128,4,1,256]{4,1,3,2,0:T(8,128)S(1)} %get-tuple-element.44), channel_id=1, source_target_pairs={{0,1},{1,2},{2,3},{4,5},{5,6},{6,7},{8,9},{9,10},{10,11},{12,13},{... | collective-permute-start | bytes 4718600 | tf_op jit(solution)/shard_map/ppermute | solution.py:15
  (51 other events, 2829.2 us)
Sparse Core Ops, SparseCore 0:
  227.9 146.9 all-reduce.14
where the time goes:
time: 638 us; the launch traced here: 628 us
  waiting for transfers between devices  372 us (58%)
  starting transfers between devices  73.5 us (12%)
  local copies, waits for them, and re-layouts  69.1 us (11%)
  blocking collectives  52.6 us (8%)
  other arithmetic  36 us (6%)
  between operations  15.8 us (2%)
  matrix products  9.54 us (1%)
    ppermute x12, waiting for transfers between devices, with_halo(): lax.ppermute(head, axis, [((i + 1) % count, i) for i in range(ends)])  160 us
    unnamed x2, waiting for transfers between devices  147 us
    ppermute x12, waiting for transfers between devices, with_halo(): lax.ppermute(tail, axis, [(i, (i + 1) % count) for i in range(ends)])  65.1 us
    ppermute x12, starting transfers between devices, with_halo(): lax.ppermute(head, axis, [((i + 1) % count, i) for i in range(ends)])  52.6 us
    all_gather x1, blocking collectives, per_device(): lax.all_gather(well_adjoint, ('slab', 'col'), axis=0, tiled=True)  52.6 us
    ppermute x12, starting transfers between devices, with_halo(): lax.ppermute(tail, axis, [(i, (i + 1) % count) for i in range(ends)])  20.9 us
    slice x7, local copies, waits for them, and re-layouts, apply_blocks(): vector[0][None]  13.2 us
  transfers between devices with their start and end apart: 25, of which 23 were waited for; matrix products, arithmetic and copies ran while one was open for 7% of the time, Pallas kernels for 0%

commit v1 on v0

v1 whole, which is shorter than its diff:
```python
import jax
import jax.numpy as jnp
from jax import lax
from jax.experimental import pallas as pl
from jax.experimental.pallas import tpu as pltpu
from jax.sharding import PartitionSpec as P

RHS = 128
LANES = 128
ROWS = 32
SLICE = 8
FACE_RX, FACE_LX, FACE_RY, FACE_LY, FACE_ZU, FACE_ZS = range(6)
SHAPE4 = jax.ShapeDtypeStruct((4, 3, RHS, LANES), jnp.float32)
SHAPE2 = jax.ShapeDtypeStruct((2, 3, RHS, LANES), jnp.float32)
COEF = jax.ShapeDtypeStruct((8, 54, LANES), jnp.float32)


def call(body, outs, args, scratch=(), flops=1_000_000, name=None):
    return pl.pallas_call(
        body,
        out_shape=outs,
        in_specs=[pl.BlockSpec(memory_space=pltpu.VMEM)] * len(args),
        out_specs=jax.tree.map(lambda _: pl.BlockSpec(memory_space=pltpu.VMEM), outs),
        scratch_shapes=list(scratch),
        compiler_params=pltpu.CompilerParams(vmem_limit_bytes=32 * 1024 * 1024),
        cost_estimate=pl.CostEstimate(flops=flops, bytes_accessed=3_000_000, transcendentals=0),
        name=name,
    )(*args)


def spots():
    return lax.rem(lax.axis_index("slab"), 2), lax.rem(lax.axis_index("col"), 2)


def line_xy(tx, ty):
    sp, cp = spots()
    x = sp if tx else 1 - sp
    y = cp if ty else 1 - cp
    return x, y


def xor(a, b):
    return a + b - 2 * a * b


def lane_iota(rows):
    return lax.broadcasted_iota(jnp.int32, (rows, LANES), 1)


def pick(values, index):
    return jnp.take_along_axis(values, index, axis=1)


def split_z(low, high, odd):
    lane = lane_iota(low.shape[0])
    index = (2 * lane + odd) & (LANES - 1)
    return jnp.where(lane < LANES // 2, pick(low, index), pick(high, index))


def join_z(even, odd, half):
    lane = lane_iota(even.shape[0])
    index = half * (LANES // 2) + (lane >> 1)
    return jnp.where((lane & 1) == 0, pick(even, index), pick(odd, index))


def line_rows(ref, start, count):
    return ref[pl.ds(start, count, stride=SLICE), :]


def tile_split(tile):
    lane = lane_iota(SLICE)
    part = (lax.broadcasted_iota(jnp.int32, (SLICE, LANES), 0) >> 1) & 1
    even = pick(tile, (2 * lane) & (LANES - 1))
    odd = pick(tile, (2 * lane + 1) & (LANES - 1))
    low = lane < LANES // 2
    of_even = jnp.where(low, even, pltpu.roll(even, SLICE - 2, 0))
    of_odd = jnp.where(low, pltpu.roll(odd, 2, 0), odd)
    return jnp.where(part == 0, of_even, of_odd)


def pivoted(rhs_ref, piv, cls, tx, ty, rows):
    x, y = line_xy(tx, ty)
    odd = xor(xor(x, y), cls)
    planes = []
    for a in range(3):
        base = (a * RHS + rows) * SLICE + x * 4 + y
        planes.append(
            split_z(line_rows(rhs_ref, base, ROWS), line_rows(rhs_ref, base + 2, ROWS), odd)
        )
    return [
        piv[0 * 3 + b] * planes[0] + piv[1 * 3 + b] * planes[1] + piv[2 * 3 + b] * planes[2]
        for b in range(3)
    ]


def class_rows(ref, cls, tx, ty, count):
    x, y = line_xy(tx, ty)
    odd = xor(xor(x, y), cls)
    return ref[pl.ds(x * 4 + odd * 2 + y, count, stride=SLICE), :]


def chunks(body):
    def step(i, carry):
        body(pl.multiple_of(i * ROWS, ROWS))
        return carry

    lax.fori_loop(0, RHS // ROWS, step, 0)


def lines():
    return [(tx, ty) for tx in range(2) for ty in range(2)]


def store_sends(outs, tx, ty, b, rows, value):
    sxa, sxb, sya, syb = outs
    (sxb if tx else sxa)[ty, b, pl.ds(rows, ROWS), :] = value
    (syb if ty else sya)[tx, b, pl.ds(rows, ROWS), :] = value


def first_kernel(rhs_ref, piv_ref, colors_ref, q_ref, sxa, sxb, sya, syb, tiles, color_tile):
    for row in range(9):
        tiles[row * 8 : row * 8 + 8, :] = tile_split(piv_ref[row * 8 : row * 8 + 8, :])
    color_tile[...] = tile_split(colors_ref[...])
    for tx, ty in lines():
        piv_rows = class_rows(tiles, 0, tx, ty, 9)
        piv = [piv_rows[i : i + 1] for i in range(9)]
        mask = class_rows(color_tile, 0, tx, ty, 1) == 0

        def body(rows, tx=tx, ty=ty, piv=piv, mask=mask):
            for b, value in enumerate(pivoted(rhs_ref, piv, 0, tx, ty, rows)):
                q_ref[tx * 2 + ty, b, pl.ds(rows, ROWS), :] = value
                store_sends((sxa, sxb, sya, syb), tx, ty, b, rows, jnp.where(mask, value, 0.0))

        chunks(body)


def add_local(acc, coef, d, tx, ty, rows, sxa, sxb, cls):
    x, y = line_xy(tx, ty)
    odd = xor(xor(x, y), cls)
    shift = 1 + odd * (LANES - 2)
    own, across = (sxb, sxa) if tx else (sxa, sxb)
    part = pl.ds(rows, ROWS)
    for a in range(3):
        center = own[ty, a, part, :]
        for face, value in (
            (FACE_LX, across[ty, a, part, :]),
            (FACE_LY, own[1 - ty, a, part, :]),
            (FACE_ZU, center),
            (FACE_ZS, pltpu.roll(center, shift, 1)),
        ):
            for b in range(3):
                row = face * 9 + a * 3 + b
                acc[b] = acc[b] - coef[d, row : row + 1, :] * value
    return acc


def add_remote(acc, coef, d, tx, ty, rows, halos):
    rxa, rxb, rya, ryb = halos
    part = pl.ds(rows, ROWS)
    for a in range(3):
        for face, value in (
            (FACE_RX, (rxb if tx else rxa)[ty, a, part, :]),
            (FACE_RY, (ryb if ty else rya)[tx, a, part, :]),
        ):
            for b in range(3):
                row = face * 9 + a * 3 + b
                acc[b] = acc[b] - coef[d, row : row + 1, :] * value
    return acc


def second_kernel(
    rhs_ref, piv_ref, colors_ref, inc_ref, sxa, sxb,
    part_ref, fwd_ref, bwd_ref, cls_colors_ref, tiles, color_tile, raw, folded,
):
    for row in range(9):
        tiles[row * 8 : row * 8 + 8, :] = tile_split(piv_ref[row * 8 : row * 8 + 8, :])
    color_tile[...] = tile_split(colors_ref[...])
    spot = lax.broadcasted_iota(jnp.int32, (SLICE, LANES), 0)
    lane = lane_iota(SLICE)
    x_low = (spot >> 2) == 0
    y_low = (spot & 1) == 0
    z_even = ((spot >> 1) & 1) == 0
    edge = (z_even & (lane == 0)) | (jnp.logical_not(z_even) & (lane == LANES - 1))

    def source(face, entry):
        row = (face * 9 + entry) * 8
        return tile_split(inc_ref[row : row + 8, :])

    piv = [tiles[i * 8 : i * 8 + 8, :] for i in range(9)]
    for group, (first, second, low) in enumerate(((0, 1, x_low), (2, 3, y_low), (5, 4, z_even))):
        one = [None] * 9
        two = [None] * 9
        for entry in range(9):
            p, q = source(first, entry), source(second, entry)
            one[entry] = jnp.where(low, p, q)
            two[entry] = jnp.where(low, q, p)
            if group == 2:
                two[entry] = jnp.where(edge, 0.0, two[entry])
        for which, block in ((0, one), (1, two)):
            face = group * 2 + which
            for a in range(3):
                for b in range(3):
                    row = (face * 9 + a * 3 + b) * 8
                    raw[row : row + 8, :] = block[a * 3 + b]
                    folded[row : row + 8, :] = (
                        block[a * 3] * piv[b]
                        + block[a * 3 + 1] * piv[3 + b]
                        + block[a * 3 + 2] * piv[6 + b]
                    )
    for cls in range(2):
        for tx, ty in lines():
            d = cls * 4 + tx * 2 + ty
            fwd_ref[d] = class_rows(folded, cls, tx, ty, 54)
            bwd_ref[d] = class_rows(raw, cls, tx, ty, 54)
            cls_colors_ref[d : d + 1, :] = class_rows(color_tile, cls, tx, ty, 1)
    for tx, ty in lines():
        d = 4 + tx * 2 + ty
        piv_rows = class_rows(tiles, 1, tx, ty, 9)
        piv1 = [piv_rows[i : i + 1] for i in range(9)]

        def body(rows, tx=tx, ty=ty, piv1=piv1, d=d):
            acc = pivoted(rhs_ref, piv1, 1, tx, ty, rows)
            acc = add_local(acc, fwd_ref, d, tx, ty, rows, sxa, sxb, 1)
            for b in range(3):
                part_ref[tx * 2 + ty, b, pl.ds(rows, ROWS), :] = acc[b]

        chunks(body)


def local_kernel(cls, base_ref, coef_ref, sxa, sxb, part_ref):
    for tx, ty in lines():
        n = tx * 2 + ty

        def body(rows, tx=tx, ty=ty, n=n):
            acc = [base_ref[n, b, pl.ds(rows, ROWS), :] for b in range(3)]
            acc = add_local(acc, coef_ref, cls * 4 + n, tx, ty, rows, sxa, sxb, cls)
            for b in range(3):
                part_ref[n, b, pl.ds(rows, ROWS), :] = acc[b]

        chunks(body)


def remote_kernel(
    cls, color, part_ref, coef_ref, colors_ref, rxa, rxb, rya, ryb, full_ref, sxa, sxb, sya, syb
):
    for tx, ty in lines():
        n = tx * 2 + ty
        d = cls * 4 + n

        def body(rows, tx=tx, ty=ty, n=n, d=d):
            acc = [part_ref[n, b, pl.ds(rows, ROWS), :] for b in range(3)]
            acc = add_remote(acc, coef_ref, d, tx, ty, rows, (rxa, rxb, rya, ryb))
            mask = colors_ref[d : d + 1, :] == color
            for b in range(3):
                full_ref[n, b, pl.ds(rows, ROWS), :] = acc[b]
                store_sends((sxa, sxb, sya, syb), tx, ty, b, rows, jnp.where(mask, acc[b], 0.0))

        chunks(body)


def perf_place(perf_cell):
    sp, cp = spots()
    x = perf_cell >> 9
    y = (perf_cell >> 8) & 1
    z = perf_cell & 255
    cls = (x + y + z) & 1
    tx = (x + 1 - sp) & 1
    ty = (y + 1 - cp) & 1
    return (cls * 4 + tx * 2 + ty) * LANES + (z >> 1)


def hot(index, start, count):
    rows = lax.broadcasted_iota(jnp.int32, (count, index.shape[1]), 0) + start
    return jnp.where(rows == index, 1.0, 0.0).astype(jnp.bfloat16)


def thirds(values):
    one = values.astype(jnp.bfloat16)
    rest = values - one.astype(jnp.float32)
    two = rest.astype(jnp.bfloat16)
    three = (rest - two.astype(jnp.float32)).astype(jnp.bfloat16)
    return one, two, three


def exact_dot(values, ones, dims):
    out = None
    for part in thirds(values):
        term = lax.dot_general(part, ones, (dims, ((), ())), preferred_element_type=jnp.float32)
        out = term if out is None else out + term
    return out


def wells_kernel(
    part_ref, t_ref, q_ref, u_ref, coef_ref, colors_ref, rxa, rxb, rya, ryb,
    perf_cell_ref, perf_well_ref, perf_out_ref, even_ref, odd_ref, sums_ref, at_ref,
):
    for tx, ty in lines():
        n = tx * 2 + ty
        d = 4 + n

        def body(rows, tx=tx, ty=ty, n=n, d=d):
            part = pl.ds(rows, ROWS)
            acc = [part_ref[n, b, part, :] for b in range(3)]
            acc = add_remote(acc, coef_ref, d, tx, ty, rows, (rxa, rxb, rya, ryb))
            is_one = colors_ref[d : d + 1, :] == 1
            is_two = colors_ref[n : n + 1, :] == 2
            for b in range(3):
                odd_ref[n, b, part, :] = jnp.where(is_one, t_ref[n, b, part, :], acc[b])
                even_ref[n, b, part, :] = jnp.where(is_two, u_ref[n, b, part, :], q_ref[n, b, part, :])

        chunks(body)
    place = perf_place(perf_cell_ref[...])
    at_perfs = None
    for cls, ref in ((0, even_ref), (1, odd_ref)):
        for n in range(4):
            planes = ref[n].reshape(3 * RHS, LANES)
            term = exact_dot(planes, hot(place, (cls * 4 + n) * LANES, LANES), ((1,), (0,)))
            at_perfs = term if at_perfs is None else at_perfs + term
    for b in range(3):
        at_ref[b * RHS : (b + 1) * RHS, :] = sum(
            perf_out_ref[a * 3 + b : a * 3 + b + 1, :] * at_perfs[a * RHS : (a + 1) * RHS]
            for a in range(3)
        )
    wells = hot(perf_well_ref[...], 0, sums_ref.shape[0])
    out = None
    for part in thirds(at_ref[...]):
        term = lax.dot_general(
            wells, part, (((1,), (1,)), ((), ())), preferred_element_type=jnp.float32
        )
        out = term if out is None else out + term
    sums_ref[...] = out


def fix_kernel(
    wells_ref, even_ref, odd_ref, colors_ref, perf_cell_ref, perf_well_ref, perf_in_ref,
    even_out, odd_out, sxa, sxb, sya, syb, at_ref,
):
    wells = wells_ref[...].T
    at_perfs = exact_dot(wells, hot(perf_well_ref[...], 0, wells.shape[1]), ((1,), (0,)))
    for b in range(3):
        at_ref[b * RHS : (b + 1) * RHS, :] = sum(
            perf_in_ref[a * 3 + b : a * 3 + b + 1, :] * at_perfs[a * RHS : (a + 1) * RHS]
            for a in range(3)
        )
    place = perf_place(perf_cell_ref[...])
    fixes = thirds(at_ref[...])
    for cls, ref, out in ((1, odd_ref, odd_out), (0, even_ref, even_out)):
        for tx, ty in lines():
            n = tx * 2 + ty
            d = cls * 4 + n
            ones = hot(place, d * LANES, LANES)
            fix = sum(
                lax.dot_general(
                    part, ones, (((1,), (1,)), ((), ())), preferred_element_type=jnp.float32
                )
                for part in fixes
            )
            for b in range(3):
                value = ref[n, b] - fix[b * RHS : (b + 1) * RHS]
                out[n, b] = value
                if cls == 1:
                    sent = jnp.where(colors_ref[d : d + 1, :] == 3, value, 0.0)
                    (sxb if tx else sxa)[ty, b] = sent
                    (syb if ty else sya)[tx, b] = sent


def last_kernel(
    part_ref, u_ref, odd_three, odd_v, coef_ref, colors_ref, rxa, rxb, rya, ryb, out_ref
):
    for tx, ty in lines():
        n = tx * 2 + ty
        x, y = line_xy(tx, ty)
        flip = xor(x, y)

        def body(rows, tx=tx, ty=ty, n=n, x=x, y=y, flip=flip):
            part = pl.ds(rows, ROWS)
            acc = [part_ref[n, b, part, :] for b in range(3)]
            acc = add_remote(acc, coef_ref, n, tx, ty, rows, (rxa, rxb, rya, ryb))
            is_two = colors_ref[n : n + 1, :] == 2
            is_one = colors_ref[4 + n : 5 + n, :] == 1
            for b in range(3):
                even = jnp.where(is_two, u_ref[n, b, part, :], acc[b])
                odd = jnp.where(is_one, odd_v[n, b, part, :], odd_three[n, b, part, :])
                z_even = jnp.where(flip == 1, odd, even)
                z_odd = jnp.where(flip == 1, even, odd)
                for half in range(2):
                    start = (b * RHS + rows) * SLICE + x * 4 + half * 2 + y
                    out_ref[pl.ds(start, ROWS, stride=SLICE), :] = join_z(z_even, z_odd, half)

        chunks(body)


def pairs(axis, second):
    count = lax.axis_size(axis)
    found = []
    for i in range(second, count - 1, 2):
        found += [(i, i + 1), (i + 1, i)]
    return found


def exchange(sends):
    sxa, sxb, sya, syb = sends
    ryb = lax.ppermute(syb, "col", pairs("col", 1))
    rya = lax.ppermute(sya, "col", pairs("col", 0))
    rxb = lax.ppermute(sxb, "slab", pairs("slab", 1))
    rxa = lax.ppermute(sxa, "slab", pairs("slab", 0))
    return rxa, rxb, rya, ryb


def well_apply(blocks, vector):
    return (
        blocks[:, 0, :, None] * vector[:, 0, None, :]
        + blocks[:, 1, :, None] * vector[:, 1, None, :]
        + blocks[:, 2, :, None] * vector[:, 2, None, :]
    )


def to_rows(array):
    lead = array.shape[:-3]
    split = array.reshape(lead + (2, 2, 2, LANES))
    return jnp.swapaxes(split, -3, -2).reshape(-1, LANES)


def from_rows(rows):
    split = rows.reshape(3, RHS, 2, 2, 2, LANES)
    return jnp.swapaxes(split, -3, -2).reshape(3, RHS, 2, 2, 2 * LANES)


def per_device(
    cell_rhs, well_rhs, cell_colors, incoming, pivot_inv,
    perf_cell, perf_well, perf_out, perf_in, well_pivot_inv,
):
    rhs = to_rows(cell_rhs)
    colors_in = to_rows(cell_colors)
    inc = to_rows(incoming)
    piv = to_rows(pivot_inv)
    perfs = perf_cell.shape[0]
    place = perf_cell.reshape(1, perfs)
    well = perf_well.reshape(1, perfs)
    out_blocks = jnp.transpose(perf_out, (1, 2, 0)).reshape(9, perfs)
    in_blocks = jnp.transpose(perf_in, (1, 2, 0)).reshape(9, perfs)
    sends = [SHAPE2] * 4
    tile_scratch = [pltpu.VMEM((72, LANES), jnp.float32), pltpu.VMEM((8, LANES), jnp.int32)]

    q_even, *s0 = call(first_kernel, [SHAPE4] + sends, (rhs, piv, colors_in), tile_scratch, name="even_rhs")
    halo = exchange(s0)
    part, fwd, bwd, colors = call(
        second_kernel,
        [SHAPE4, COEF, COEF, jax.ShapeDtypeStruct((8, LANES), jnp.int32)],
        (rhs, piv, colors_in, inc, s0[0], s0[1]),
        tile_scratch + [pltpu.VMEM((54 * 8, LANES), jnp.float32)] * 2,
        name="blocks_and_local",
    )

    def local(cls, base, coef, s, name):
        def body(*refs):
            local_kernel(cls, *refs)

        return call(body, SHAPE4, (base, coef, s[0], s[1]), name=name)

    def remote(cls, color, part, coef, halo, name):
        def body(*refs):
            remote_kernel(cls, color, *refs)

        full, *s = call(body, [SHAPE4] + sends, (part, coef, colors) + tuple(halo), name=name)
        return full, s

    t_odd, s1 = remote(1, 1, part, fwd, halo, "forward_one")
    halo = exchange(s1)
    part = local(0, q_even, fwd, s1, "forward_two_local")
    u_even, s2 = remote(0, 2, part, fwd, halo, "forward_two")
    halo = exchange(s2)
    part = local(1, t_odd, fwd, s2, "forward_three_local")
    own_count = well_pivot_inv.shape[0]
    well_count = lax.axis_size(("slab", "col")) * own_count
    devices = well_count // own_count
    even, odd, sums = call(
        wells_kernel,
        [SHAPE4, SHAPE4, jax.ShapeDtypeStruct((well_count, 3 * RHS), jnp.float32)],
        (part, t_odd, q_even, u_even, fwd, colors) + tuple(halo) + (place, well, out_blocks),
        [pltpu.VMEM((3 * RHS, perfs), jnp.float32)],
        name="forward_three_wells",
    )
    axes = ("slab", "col")
    parts = lax.all_to_all(
        sums.reshape(devices, own_count * 3, RHS), axes, 0, 0, tiled=True
    )
    own_sum = jnp.sum(parts, axis=0).reshape(own_count, 3, RHS)
    well_adjoint = well_apply(well_pivot_inv, well_rhs - own_sum)
    spread = jnp.broadcast_to(well_adjoint.reshape(1, own_count * 3, RHS), (devices, own_count * 3, RHS))
    all_wells = lax.all_to_all(spread, axes, 0, 0, tiled=True).reshape(well_count, 3 * RHS)
    x_even, x_odd, *s3 = call(
        fix_kernel,
        [SHAPE4, SHAPE4] + sends,
        (all_wells, even, odd, colors, place, well, in_blocks),
        [pltpu.VMEM((3 * RHS, perfs), jnp.float32)],
        name="well_fix",
    )
    halo = exchange(s3)
    part = local(0, x_even, bwd, s3, "backward_two_local")
    u_even, s4 = remote(0, 2, part, bwd, halo, "backward_two")
    halo = exchange(s4)
    part = local(1, x_odd, bwd, s4, "backward_one_local")
    v_odd, s5 = remote(1, 1, part, bwd, halo, "backward_one")
    halo = exchange(s5)
    part = local(0, u_even, bwd, s5, "backward_zero_local")
    rows = call(
        last_kernel,
        jax.ShapeDtypeStruct((3 * RHS * SLICE, LANES), jnp.float32),
        (part, u_even, x_odd, v_odd, bwd, colors) + tuple(halo),
        name="backward_zero",
    )
    return from_rows(rows), well_adjoint


def solution(mesh):
    placed = (
        P(None, None, "slab", "col", None),
        P(("slab", "col"), None, None),
        P("slab", "col", None),
        P(None, None, None, "slab", "col", None),
        P(None, None, "slab", "col", None),
        P(("slab", "col")),
        P(("slab", "col")),
        P(("slab", "col"), None, None),
        P(("slab", "col"), None, None),
        P(("slab", "col"), None, None),
    )
    return jax.shard_map(
        per_device,
        mesh=mesh,
        in_specs=placed,
        out_specs=(P(None, None, "slab", "col", None), P(("slab", "col"), None, None)),
        check_vma=False,
    )
```

time: 638 us -> 165 us (0.26)
  the two profiles are of different devices: /device:TPU:38 before, /device:TPU:24 now
where the time goes in v1:
time: 165 us; the launch traced here: 162 us
  waiting for transfers between devices  62.6 us (38%)
  starting transfers between devices  57.9 us (35%)
  Pallas kernels  27.6 us (17%)
  local copies, waits for them, and re-layouts  11.8 us (7%)
    ppermute x6, waiting for transfers between devices, exchange(): rya = lax.ppermute(sya, 'col', pairs('col', 0))  32.8 us
    pallas_call x14, Pallas kernels, call(): pl.pallas_call(body, out_shape=outs, in_specs=[pl.BlockSpec(memory_space=...  27.6 us
    ppermute x6, starting transfers between devices, exchange(): rya = lax.ppermute(sya, 'col', pairs('col', 0))  18.4 us
    ppermute x6, starting transfers between devices, exchange(): rxb = lax.ppermute(sxb, 'slab', pairs('slab', 1))  15.8 us
    all_to_all x1, starting transfers between devices, per_device(): lax.all_to_all(sums.reshape(devices, own_count * 3, RHS), axes, 0, 0, til...  12.4 us
    all_to_all x1, waiting for transfers between devices, per_device(): lax.all_to_all(spread, axes, 0, 0, tiled=True).reshape(well_count, 3 * RHS)  12.2 us
    all_to_all x1, waiting for transfers between devices, per_device(): lax.all_to_all(sums.reshape(devices, own_count * 3, RHS), axes, 0, 0, til...  12 us
    unnamed x38, local copies, waits for them, and re-layouts  8.32 us
  transfers between devices with their start and end apart: 26, of which 12 were waited for; matrix products, arithmetic and copies ran while one was open for 1% of the time, Pallas kernels for 8%

profile of v1, /device:TPU:24, one launch (start us, length us, event | category | flops | bytes accessed | tf_op | source)
XLA Modules:
  0.0 161.9 jit_solution(15316698189782465282)
XLA Ops:
  3.5 1.8 %even_rhs.1 = (f32[4,3,128,128]{3,2,1,0:T(8,128)S(1)}, f32[2,3,128,128]{3,2,1,0:T(8,128)S(1)}, f32[2,3,128,128]{3,2,1,0:T(8,128)S(1)}, f32[2,3,128,128]{3,2,1,0:T(8,128)S(1)}, f32[2,3,128,128]{3,2,1,0:T(8,128)S(1)}) custom-call(f32[3072,128]{1,0:T(8,128)S(1)} %bitcast.44, f32[72,128]{1,0:T(8,128)S(1)} %bitcast.47, s32[8,128]{1,0:T(8,128)S(1)} %bitcast.49), custom_call_target="tpu_custom_call" | custom-call | flops 1000000 | bytes 3000000 | tf_op jit(solution)/shard_map/even_rhs/pallas_call | solution.py:19
  5.4 2.7 %collective-permute-start.1 = (f32[2,3,128,128]{3,2,1,0:T(8,128)S(1)}, f32[2,3,128,128]{3,2,1,0:T(8,128)S(1)}, u32[]{:S(2)}, u32[]{:S(2)}) collective-permute-start(f32[2,3,128,128]{3,2,1,0:T(8,128)S(1)} %get-tuple-element.41.sxb), channel_id=1, source_target_pairs={{4,8},{8,4},{12,16},{16,12},{20,24},{24,20},{28,32},{32,28},{36,40... | collective-permute-start | bytes 1179656 | tf_op jit(solution)/shard_map/ppermute | solution.py:405
  10.5 2.4 %blocks_and_local.1 = (f32[4,3,128,128]{3,2,1,0:T(8,128)S(1)}, f32[8,54,128]{2,1,0:T(8,128)S(1)}, f32[8,54,128]{2,1,0:T(8,128)S(1)}, s32[8,128]{1,0:T(8,128)S(1)}) custom-call(f32[3072,128]{1,0:T(8,128)S(1)} %bitcast.45, f32[72,128]{1,0:T(8,128)S(1)} %bitcast.48, s32[8,128]{1,0:T(8,128)S(1)} %bitcast.50, f32[432,128]{1,0:T(8,128)S(1)} %bitcast.46, ...), custom_call_target="tpu_custom_call" | custom-call | flops 1000000 | bytes 3000000 | tf_op jit(solution)/shard_map/blocks_and_local/pallas_call | solution.py:19
  12.8 1.7 %collective-permute-done.1.refs_4_ = f32[2,3,128,128]{3,2,1,0:T(8,128)S(1)} collective-permute-done((f32[2,3,128,128]{3,2,1,0:T(8,128)S(1)}, f32[2,3,128,128]{3,2,1,0:T(8,128)S(1)}, u32[]{:S(2)}, u32[]{:S(2)}) %collective-permute-start.1) | collective-permute-done | bytes 393248 | tf_op jit(solution)/shard_map/ppermute | solution.py:405
  14.5 5.6 %collective-permute-done.2.refs_5_ = f32[2,3,128,128]{3,2,1,0:T(8,128)S(1)} collective-permute-done((f32[2,3,128,128]{3,2,1,0:T(8,128)S(1)}, f32[2,3,128,128]{3,2,1,0:T(8,128)S(1)}, u32[]{:S(2)}, u32[]{:S(2)}) %collective-permute-start.2) | collective-permute-done | bytes 393248 | tf_op jit(solution)/shard_map/ppermute | solution.py:404
  20.7 2.4 %collective-permute-start.5 = (f32[2,3,128,128]{3,2,1,0:T(8,128)S(1)}, f32[2,3,128,128]{3,2,1,0:T(8,128)S(1)}, u32[]{:S(2)}, u32[]{:S(2)}) collective-permute-start(f32[2,3,128,128]{3,2,1,0:T(8,128)S(1)} %get-tuple-element.50.refs_3_), channel_id=1, source_target_pairs={{4,8},{8,4},{12,16},{16,12},{20,24},{24,20},{28,32},{32,28},{36,40... | collective-permute-start | bytes 1179656 | tf_op jit(solution)/shard_map/ppermute | solution.py:405
  23.2 4.1 %collective-permute-start.6 = (f32[2,3,128,128]{3,2,1,0:T(8,128)S(1)}, f32[2,3,128,128]{3,2,1,0:T(8,128)S(1)}, u32[]{:S(2)}, u32[]{:S(2)}) collective-permute-start(f32[2,3,128,128]{3,2,1,0:T(8,128)S(1)} %get-tuple-element.51), channel_id=1, source_target_pairs={{0,1},{1,0},{2,3},{3,2},{4,5},{5,4},{6,7},{7,6},{8,9},{9,8},{10,11... | collective-permute-start | bytes 1179656 | tf_op jit(solution)/shard_map/ppermute | solution.py:404
  28.0 1.6 %forward_two_local.1.refs_0_ = f32[4,3,128,128]{3,2,1,0:T(8,128)S(1)} custom-call(f32[4,3,128,128]{3,2,1,0:T(8,128)S(1)} %get-tuple-element.48.refs_0_.q_ref, f32[8,54,128]{2,1,0:T(8,128)S(1)} %get-tuple-element.43.refs_1_.coef_ref, f32[2,3,128,128]{3,2,1,0:T(8,128)S(1)} %get-tuple-element.49.refs_2_, f32[2,3,128,128]{3,2,1,0:T(8,128)S(1)} %get-tuple-element.50.refs_3_), custom_call_target="tpu_custom_call" | custom-call | flops 1000000 | bytes 3000000 | tf_op jit(solution)/shard_map/forward_two_local/pallas_call | solution.py:19
  29.8 7.1 %collective-permute-done.6.refs_5_ = f32[2,3,128,128]{3,2,1,0:T(8,128)S(1)} collective-permute-done((f32[2,3,128,128]{3,2,1,0:T(8,128)S(1)}, f32[2,3,128,128]{3,2,1,0:T(8,128)S(1)}, u32[]{:S(2)}, u32[]{:S(2)}) %collective-permute-start.6) | collective-permute-done | bytes 393248 | tf_op jit(solution)/shard_map/ppermute | solution.py:404
  39.2 4.1 %collective-permute-start.10 = (f32[2,3,128,128]{3,2,1,0:T(8,128)}, f32[2,3,128,128]{3,2,1,0:T(8,128)S(1)}, u32[]{:S(2)}, u32[]{:S(2)}) collective-permute-start(f32[2,3,128,128]{3,2,1,0:T(8,128)} %get-tuple-element.56), channel_id=1, source_target_pairs={{0,1},{1,0},{2,3},{3,2},{4,5},{5,4},{6,7},{7,6},{8,9},{9,8},{10,11... | collective-permute-start | bytes 1179656 | tf_op jit(solution)/shard_map/ppermute | solution.py:404
  44.1 2.5 %collective-permute-start.9 = (f32[2,3,128,128]{3,2,1,0:T(8,128)S(1)}, f32[2,3,128,128]{3,2,1,0:T(8,128)}, u32[]{:S(2)}, u32[]{:S(2)}) collective-permute-start(f32[2,3,128,128]{3,2,1,0:T(8,128)S(1)} %get-tuple-element.54.refs_3_), channel_id=1, source_target_pairs={{4,8},{8,4},{12,16},{16,12},{20,24},{24,20},{28,32},{32,28},{36,40... | collective-permute-start | bytes 1179656 | tf_op jit(solution)/shard_map/ppermute | solution.py:405
  46.7 2.7 %forward_three_local.1.part_ref = f32[4,3,128,128]{3,2,1,0:T(8,128)S(1)} custom-call(f32[4,3,128,128]{3,2,1,0:T(8,128)S(1)} %get-tuple-element.47.refs_0_.t_ref, f32[8,54,128]{2,1,0:T(8,128)S(1)} %get-tuple-element.43.refs_1_.coef_ref, f32[2,3,128,128]{3,2,1,0:T(8,128)} %get-tuple-element.53.refs_2_, f32[2,3,128,128]{3,2,1,0:T(8,128)S(1)} %get-tuple-element.54.refs_3_), custom_call_target="tpu_custom_call" | custom-call | flops 1000000 | bytes 3000000 | tf_op jit(solution)/shard_map/forward_three_local/pallas_call | solution.py:19
  49.4 3.6 %collective-permute-done.10.rya = f32[2,3,128,128]{3,2,1,0:T(8,128)S(1)} collective-permute-done((f32[2,3,128,128]{3,2,1,0:T(8,128)}, f32[2,3,128,128]{3,2,1,0:T(8,128)S(1)}, u32[]{:S(2)}, u32[]{:S(2)}) %collective-permute-start.10) | collective-permute-done | bytes 393248 | tf_op jit(solution)/shard_map/ppermute | solution.py:404
  54.8 3.0 %forward_three_wells.1 = (f32[4,3,128,128]{3,2,1,0:T(8,128)S(1)}, f32[4,3,128,128]{3,2,1,0:T(8,128)S(1)}, f32[256,384]{1,0:T(8,128)S(1)}) custom-call(f32[4,3,128,128]{3,2,1,0:T(8,128)S(1)} %forward_three_local.1.part_ref, f32[4,3,128,128]{3,2,1,0:T(8,128)S(1)} %get-tuple-element.47.refs_0_.t_ref, f32[4,3,128,128]{3,2,1,0:T(8,128)S(1)} %get-tuple-element.48.refs_0_.q_ref, ...), custom_call_target="tpu_custom_call" | custom-call | flops 1000000 | bytes 3000000 | tf_op jit(solution)/shard_map/forward_three_wells/pallas_call | solution.py:19
  59.4 1.9 %reshape.117 = f32[128,6,128]{2,1,0:T(8,128)} reshape(f32[256,384]{1,0:T(8,128)} %copy-done.7) | data formatting | bytes 786432 | tf_op jit(solution)/shard_map/reshape | solution.py:486
  61.4 12.4 %all-to-all-start = ((f32[128,6,128]{2,1,0:T(8,128)}), f32[128,6,128]{2,1,0:T(8,128)S(1)}, u32[]{:S(2)}, u32[]{:S(2)}) async-start(f32[128,6,128]{2,1,0:T(8,128)} %reshape.117), calls=%async_computation | async-start | bytes 1048576 | tf_op jit(solution)/shard_map/all_to_all | solution.py:485
  74.0 12.0 %all-to-all-done = f32[128,6,128]{2,1,0:T(8,128)S(1)} async-done(((f32[128,6,128]{2,1,0:T(8,128)}), f32[128,6,128]{2,1,0:T(8,128)S(1)}, u32[]{:S(2)}, u32[]{:S(2)}) %all-to-all-start) | async-done | bytes 393248 | tf_op jit(solution)/shard_map/all_to_all | solution.py:485
  87.1 5.7 %all-to-all-start.1 = ((f32[128,6,128]{2,1,0:T(8,128)}), f32[128,6,128]{2,1,0:T(8,128)S(1)}, u32[]{:S(2)}, u32[]{:S(2)}) async-start(f32[128,6,128]{2,1,0:T(8,128)} %broadcast_in_dim.2), calls=%async_computation.1 | async-start | bytes 1048576 | tf_op jit(solution)/shard_map/all_to_all | solution.py:491
  92.9 12.2 %all-to-all-done.1 = f32[128,6,128]{2,1,0:T(8,128)S(1)} async-done(((f32[128,6,128]{2,1,0:T(8,128)}), f32[128,6,128]{2,1,0:T(8,128)S(1)}, u32[]{:S(2)}, u32[]{:S(2)}) %all-to-all-start.1) | async-done | bytes 393248 | tf_op jit(solution)/shard_map/all_to_all | solution.py:491
  107.8 3.0 %collective-permute-start.13 = (f32[2,3,128,128]{3,2,1,0:T(8,128)S(1)}, f32[2,3,128,128]{3,2,1,0:T(8,128)S(1)}, u32[]{:S(2)}, u32[]{:S(2)}) collective-permute-start(f32[2,3,128,128]{3,2,1,0:T(8,128)S(1)} %get-tuple-element.64.refs_3_), channel_id=1, source_target_pairs={{4,8},{8,4},{12,16},{16,12},{20,24},{24,20},{28,32},{32,28},{36,40... | collective-permute-start | bytes 1179656 | tf_op jit(solution)/shard_map/ppermute | solution.py:405
  112.2 1.6 %backward_two_local.1.refs_0_ = f32[4,3,128,128]{3,2,1,0:T(8,128)S(1)} custom-call(f32[4,3,128,128]{3,2,1,0:T(8,128)S(1)} %get-tuple-element.61.refs_0_, f32[8,54,128]{2,1,0:T(8,128)S(1)} %get-tuple-element.62.refs_1_.coef_ref, f32[2,3,128,128]{3,2,1,0:T(8,128)S(1)} %get-tuple-element.63.refs_2_, f32[2,3,128,128]{3,2,1,0:T(8,128)S(1)} %get-tuple-element.64.refs_3_), custom_call_target="tpu_custom_call" | custom-call | flops 1000000 | bytes 3000000 | tf_op jit(solution)/shard_map/backward_two_local/pallas_call | solution.py:19
  113.8 3.1 %collective-permute-done.13.refs_4_ = f32[2,3,128,128]{3,2,1,0:T(8,128)S(1)} collective-permute-done((f32[2,3,128,128]{3,2,1,0:T(8,128)S(1)}, f32[2,3,128,128]{3,2,1,0:T(8,128)S(1)}, u32[]{:S(2)}, u32[]{:S(2)}) %collective-permute-start.13) | collective-permute-done | bytes 393248 | tf_op jit(solution)/shard_map/ppermute | solution.py:405
  116.9 5.4 %collective-permute-done.14.refs_5_ = f32[2,3,128,128]{3,2,1,0:T(8,128)S(1)} collective-permute-done((f32[2,3,128,128]{3,2,1,0:T(8,128)S(1)}, f32[2,3,128,128]{3,2,1,0:T(8,128)S(1)}, u32[]{:S(2)}, u32[]{:S(2)}) %collective-permute-start.14) | collective-permute-done | bytes 393248 | tf_op jit(solution)/shard_map/ppermute | solution.py:404
  123.2 2.3 %collective-permute-start.17 = (f32[2,3,128,128]{3,2,1,0:T(8,128)S(1)}, f32[2,3,128,128]{3,2,1,0:T(8,128)S(1)}, u32[]{:S(2)}, u32[]{:S(2)}) collective-permute-start(f32[2,3,128,128]{3,2,1,0:T(8,128)S(1)} %get-tuple-element.70.refs_3_), channel_id=1, source_target_pairs={{4,8},{8,4},{12,16},{16,12},{20,24},{24,20},{28,32},{32,28},{36,40... | collective-permute-start | bytes 1179656 | tf_op jit(solution)/shard_map/ppermute | solution.py:405
  125.6 3.7 %collective-permute-start.18 = (f32[2,3,128,128]{3,2,1,0:T(8,128)S(1)}, f32[2,3,128,128]{3,2,1,0:T(8,128)S(1)}, u32[]{:S(2)}, u32[]{:S(2)}) collective-permute-start(f32[2,3,128,128]{3,2,1,0:T(8,128)S(1)} %get-tuple-element.71), channel_id=1, source_target_pairs={{0,1},{1,0},{2,3},{3,2},{4,5},{5,4},{6,7},{7,6},{8,9},{9,8},{10,11... | collective-permute-start | bytes 1179656 | tf_op jit(solution)/shard_map/ppermute | solution.py:404
  130.0 1.7 %backward_one_local.1.refs_0_ = f32[4,3,128,128]{3,2,1,0:T(8,128)S(1)} custom-call(f32[4,3,128,128]{3,2,1,0:T(8,128)S(1)} %get-tuple-element.68.refs_0_.odd_three, f32[8,54,128]{2,1,0:T(8,128)S(1)} %get-tuple-element.62.refs_1_.coef_ref, f32[2,3,128,128]{3,2,1,0:T(8,128)S(1)} %get-tuple-element.69.refs_2_, f32[2,3,128,128]{3,2,1,0:T(8,128)S(1)} %get-tuple-element.70.refs_3_), custom_call_target="tpu_custom_call" | custom-call | flops 1000000 | bytes 3000000 | tf_op jit(solution)/shard_map/backward_one_local/pallas_call | solution.py:19
  132.3 6.6 %collective-permute-done.18.refs_5_ = f32[2,3,128,128]{3,2,1,0:T(8,128)S(1)} collective-permute-done((f32[2,3,128,128]{3,2,1,0:T(8,128)S(1)}, f32[2,3,128,128]{3,2,1,0:T(8,128)S(1)}, u32[]{:S(2)}, u32[]{:S(2)}) %collective-permute-start.18) | collective-permute-done | bytes 393248 | tf_op jit(solution)/shard_map/ppermute | solution.py:404
  140.7 2.9 %collective-permute-start.21 = (f32[2,3,128,128]{3,2,1,0:T(8,128)}, f32[2,3,128,128]{3,2,1,0:T(8,128)S(1)}, u32[]{:S(2)}, u32[]{:S(2)}) collective-permute-start(f32[2,3,128,128]{3,2,1,0:T(8,128)} %get-tuple-element.74.refs_3_), channel_id=1, source_target_pairs={{4,8},{8,4},{12,16},{16,12},{20,24},{24,20},{28,32},{32,28},{36,40... | collective-permute-start | bytes 1179656 | tf_op jit(solution)/shard_map/ppermute | solution.py:405
  143.6 4.2 %collective-permute-start.22 = (f32[2,3,128,128]{3,2,1,0:T(8,128)}, f32[2,3,128,128]{3,2,1,0:T(8,128)}, u32[]{:S(2)}, u32[]{:S(2)}) collective-permute-start(f32[2,3,128,128]{3,2,1,0:T(8,128)} %get-tuple-element.76), channel_id=1, source_target_pairs={{0,1},{1,0},{2,3},{3,2},{4,5},{5,4},{6,7},{7,6},{8,9},{9,8},{10,11... | collective-permute-start | bytes 1179656 | tf_op jit(solution)/shard_map/ppermute | solution.py:404
  150.1 2.8 %backward_zero_local.1.part_ref = f32[4,3,128,128]{3,2,1,0:T(8,128)S(1)} custom-call(f32[4,3,128,128]{3,2,1,0:T(8,128)S(1)} %get-tuple-element.67.refs_0_.u_ref, f32[8,54,128]{2,1,0:T(8,128)S(1)} %get-tuple-element.62.refs_1_.coef_ref, f32[2,3,128,128]{3,2,1,0:T(8,128)} %get-tuple-element.73.refs_2_, f32[2,3,128,128]{3,2,1,0:T(8,128)} %get-tuple-element.74.refs_3_), custom_call_target="tpu_custom_call" | custom-call | flops 1000000 | bytes 3000000 | tf_op jit(solution)/shard_map/backward_zero_local/pallas_call | solution.py:19
  152.9 4.5 %collective-permute-done.22.rya = f32[2,3,128,128]{3,2,1,0:T(8,128)} collective-permute-done((f32[2,3,128,128]{3,2,1,0:T(8,128)}, f32[2,3,128,128]{3,2,1,0:T(8,128)}, u32[]{:S(2)}, u32[]{:S(2)}) %collective-permute-start.22) | collective-permute-done | bytes 393248 | tf_op jit(solution)/shard_map/ppermute | solution.py:404
  157.4 4.6 %backward_zero.1 = f32[3072,128]{1,0:T(8,128)} custom-call(f32[4,3,128,128]{3,2,1,0:T(8,128)S(1)} %backward_zero_local.1.part_ref, f32[4,3,128,128]{3,2,1,0:T(8,128)S(1)} %get-tuple-element.67.refs_0_.u_ref, f32[4,3,128,128]{3,2,1,0:T(8,128)S(1)} %get-tuple-element.68.refs_0_.odd_three, f32[4,3,128,128]{3,2,1,0:T(8,128)S(1)} %get-tuple-element.75.odd_v, ...), custom_call_target="tpu_custom_call" | custom-call | flops 1000000 | bytes 3000000 | tf_op jit(solution)/shard_map/backward_zero/pallas_call | solution.py:19
  (96 shorter events, 25.0 us)
Async XLA Ops:
  5.3 7.5 %collective-permute-start = (f32[2,3,128,128]{3,2,1,0:T(8,128)S(1)}, f32[2,3,128,128]{3,2,1,0:T(8,128)S(1)}, u32[]{:S(2)}, u32[]{:S(2)}) collective-permute-start(f32[2,3,128,128]{3,2,1,0:T(8,128)S(1)} %get-tuple-element.40.sxa), channel_id=1, source_target_pairs={{0,4},{4,0},{8,12},{12,8},{16,20},{20,16},{24,28},{28,24},{32,36},... | collective-permute-start | bytes 1179656 | tf_op jit(solution)/shard_map/ppermute | solution.py:406
  5.4 9.1 %collective-permute-start.1 = (f32[2,3,128,128]{3,2,1,0:T(8,128)S(1)}, f32[2,3,128,128]{3,2,1,0:T(8,128)S(1)}, u32[]{:S(2)}, u32[]{:S(2)}) collective-permute-start(f32[2,3,128,128]{3,2,1,0:T(8,128)S(1)} %get-tuple-element.41.sxb), channel_id=1, source_target_pairs={{4,8},{8,4},{12,16},{16,12},{20,24},{24,20},{28,32},{32,28},{36,40... | collective-permute-start | bytes 1179656 | tf_op jit(solution)/shard_map/ppermute | solution.py:405
  8.2 12.0 %collective-permute-start.2 = (f32[2,3,128,128]{3,2,1,0:T(8,128)S(1)}, f32[2,3,128,128]{3,2,1,0:T(8,128)S(1)}, u32[]{:S(2)}, u32[]{:S(2)}) collective-permute-start(f32[2,3,128,128]{3,2,1,0:T(8,128)S(1)} %get-tuple-element.45), channel_id=1, source_target_pairs={{0,1},{1,0},{2,3},{3,2},{4,5},{5,4},{6,7},{7,6},{8,9},{9,8},{10,11... | collective-permute-start | bytes 1179656 | tf_op jit(solution)/shard_map/ppermute | solution.py:404
  9.7 10.4 %collective-permute-start.3 = (f32[2,3,128,128]{3,2,1,0:T(8,128)S(1)}, f32[2,3,128,128]{3,2,1,0:T(8,128)S(1)}, u32[]{:S(2)}, u32[]{:S(2)}) collective-permute-start(f32[2,3,128,128]{3,2,1,0:T(8,128)S(1)} %get-tuple-element.46), channel_id=1, source_target_pairs={{1,2},{2,1},{5,6},{6,5},{9,10},{10,9},{13,14},{14,13},{17,18},{18,... | collective-permute-start | bytes 1179656 | tf_op jit(solution)/shard_map/ppermute | solution.py:403
  20.6 9.0 %collective-permute-start.4 = (f32[2,3,128,128]{3,2,1,0:T(8,128)S(1)}, f32[2,3,128,128]{3,2,1,0:T(8,128)S(1)}, u32[]{:S(2)}, u32[]{:S(2)}) collective-permute-start(f32[2,3,128,128]{3,2,1,0:T(8,128)S(1)} %get-tuple-element.49.refs_2_), channel_id=1, source_target_pairs={{0,4},{4,0},{8,12},{12,8},{16,20},{20,16},{24,28},{28,24},{32,36},... | collective-permute-start | bytes 1179656 | tf_op jit(solution)/shard_map/ppermute | solution.py:406
  20.7 9.1 %collective-permute-start.5 = (f32[2,3,128,128]{3,2,1,0:T(8,128)S(1)}, f32[2,3,128,128]{3,2,1,0:T(8,128)S(1)}, u32[]{:S(2)}, u32[]{:S(2)}) collective-permute-start(f32[2,3,128,128]{3,2,1,0:T(8,128)S(1)} %get-tuple-element.50.refs_3_), channel_id=1, source_target_pairs={{4,8},{8,4},{12,16},{16,12},{20,24},{24,20},{28,32},{32,28},{36,40... | collective-permute-start | bytes 1179656 | tf_op jit(solution)/shard_map/ppermute | solution.py:405
  23.2 13.7 %collective-permute-start.6 = (f32[2,3,128,128]{3,2,1,0:T(8,128)S(1)}, f32[2,3,128,128]{3,2,1,0:T(8,128)S(1)}, u32[]{:S(2)}, u32[]{:S(2)}) collective-permute-start(f32[2,3,128,128]{3,2,1,0:T(8,128)S(1)} %get-tuple-element.51), channel_id=1, source_target_pairs={{0,1},{1,0},{2,3},{3,2},{4,5},{5,4},{6,7},{7,6},{8,9},{9,8},{10,11... | collective-permute-start | bytes 1179656 | tf_op jit(solution)/shard_map/ppermute | solution.py:404
  27.3 9.6 %collective-permute-start.7 = (f32[2,3,128,128]{3,2,1,0:T(8,128)S(1)}, f32[2,3,128,128]{3,2,1,0:T(8,128)S(1)}, u32[]{:S(2)}, u32[]{:S(2)}) collective-permute-start(f32[2,3,128,128]{3,2,1,0:T(8,128)S(1)} %get-tuple-element.52), channel_id=1, source_target_pairs={{1,2},{2,1},{5,6},{6,5},{9,10},{10,9},{13,14},{14,13},{17,18},{18,... | collective-permute-start | bytes 1179656 | tf_op jit(solution)/shard_map/ppermute | solution.py:403
  29.6 17.0 %copy-start.15 = (f32[64,3,3]{0,2,1:T(4,128)S(1)}, f32[64,3,3]{0,2,1:T(4,128)}, u32[]{:S(2)}) copy-start(f32[64,3,3]{0,2,1:T(4,128)} %param.17) | copy-start | bytes 6916
  39.2 14.5 %copy-start.13 = (s32[64]{0:T(128)S(1)}, s32[64]{0:T(128)}, u32[]{:S(2)}) copy-start(s32[64]{0:T(128)} %param.15) | copy-start | bytes 772
  39.2 14.5 %copy-start.14 = (s32[64]{0:T(128)S(1)}, s32[64]{0:T(128)}, u32[]{:S(2)}) copy-start(s32[64]{0:T(128)} %param.16) | copy-start | bytes 772
  39.2 13.7 %collective-permute-start.10 = (f32[2,3,128,128]{3,2,1,0:T(8,128)}, f32[2,3,128,128]{3,2,1,0:T(8,128)S(1)}, u32[]{:S(2)}, u32[]{:S(2)}) collective-permute-start(f32[2,3,128,128]{3,2,1,0:T(8,128)} %get-tuple-element.56), channel_id=1, source_target_pairs={{0,1},{1,0},{2,3},{3,2},{4,5},{5,4},{6,7},{7,6},{8,9},{9,8},{10,11... | collective-permute-start | bytes 1179656 | tf_op jit(solution)/shard_map/ppermute | solution.py:404
  43.4 9.6 %collective-permute-start.11 = (f32[2,3,128,128]{3,2,1,0:T(8,128)}, f32[2,3,128,128]{3,2,1,0:T(8,128)S(1)}, u32[]{:S(2)}, u32[]{:S(2)}) collective-permute-start(f32[2,3,128,128]{3,2,1,0:T(8,128)} %get-tuple-element.57), channel_id=1, source_target_pairs={{1,2},{2,1},{5,6},{6,5},{9,10},{10,9},{13,14},{14,13},{17,18},{18,... | collective-permute-start | bytes 1179656 | tf_op jit(solution)/shard_map/ppermute | solution.py:403
  44.0 9.7 %collective-permute-start.8 = (f32[2,3,128,128]{3,2,1,0:T(8,128)}, f32[2,3,128,128]{3,2,1,0:T(8,128)}, u32[]{:S(2)}, u32[]{:S(2)}) collective-permute-start(f32[2,3,128,128]{3,2,1,0:T(8,128)} %get-tuple-element.53.refs_2_), channel_id=1, source_target_pairs={{0,4},{4,0},{8,12},{12,8},{16,20},{20,16},{24,28},{28,24},{32,36},... | collective-permute-start | bytes 1179656 | tf_op jit(solution)/shard_map/ppermute | solution.py:406
  44.1 9.6 %collective-permute-start.9 = (f32[2,3,128,128]{3,2,1,0:T(8,128)S(1)}, f32[2,3,128,128]{3,2,1,0:T(8,128)}, u32[]{:S(2)}, u32[]{:S(2)}) collective-permute-start(f32[2,3,128,128]{3,2,1,0:T(8,128)S(1)} %get-tuple-element.54.refs_3_), channel_id=1, source_target_pairs={{4,8},{8,4},{12,16},{16,12},{20,24},{24,20},{28,32},{32,28},{36,40... | collective-permute-start | bytes 1179656 | tf_op jit(solution)/shard_map/ppermute | solution.py:405
  59.4 14.3 %copy-start.17 = (f32[2,3,3]{2,0,1:T(2,128)S(1)}, f32[2,3,3]{2,0,1:T(2,128)}, u32[]{:S(2)}) copy-start(f32[2,3,3]{2,0,1:T(2,128)} %param.19) | copy-start | bytes 220
  59.4 26.7 %copy-start.18 = (f32[2,3,128]{2,0,1:T(2,128)S(1)}, f32[2,3,128]{2,0,1:T(2,128)}, u32[]{:S(2)}) copy-start(f32[2,3,128]{2,0,1:T(2,128)} %param.11) | copy-start | bytes 9220
  61.4 31.5 %copy-start.16 = (f32[64,3,3]{0,2,1:T(4,128)S(1)}, f32[64,3,3]{0,2,1:T(4,128)}, u32[]{:S(2)}) copy-start(f32[64,3,3]{0,2,1:T(4,128)} %param.18) | copy-start | bytes 6916
  61.4 24.6 %all-to-all-start = ((f32[128,6,128]{2,1,0:T(8,128)}), f32[128,6,128]{2,1,0:T(8,128)S(1)}, u32[]{:S(2)}, u32[]{:S(2)}) async-start(f32[128,6,128]{2,1,0:T(8,128)} %reshape.117), calls=%async_computation | async-start | bytes 1048576 | tf_op jit(solution)/shard_map/all_to_all | solution.py:485
  87.1 17.9 %all-to-all-start.1 = ((f32[128,6,128]{2,1,0:T(8,128)}), f32[128,6,128]{2,1,0:T(8,128)S(1)}, u32[]{:S(2)}, u32[]{:S(2)}) async-start(f32[128,6,128]{2,1,0:T(8,128)} %broadcast_in_dim.2), calls=%async_computation.1 | async-start | bytes 1048576 | tf_op jit(solution)/shard_map/all_to_all | solution.py:491
  107.7 6.1 %collective-permute-start.12 = (f32[2,3,128,128]{3,2,1,0:T(8,128)S(1)}, f32[2,3,128,128]{3,2,1,0:T(8,128)S(1)}, u32[]{:S(2)}, u32[]{:S(2)}) collective-permute-start(f32[2,3,128,128]{3,2,1,0:T(8,128)S(1)} %get-tuple-element.63.refs_2_), channel_id=1, source_target_pairs={{0,4},{4,0},{8,12},{12,8},{16,20},{20,16},{24,28},{28,24},{32,36},... | collective-permute-start | bytes 1179656 | tf_op jit(solution)/shard_map/ppermute | solution.py:406
  107.8 9.1 %collective-permute-start.13 = (f32[2,3,128,128]{3,2,1,0:T(8,128)S(1)}, f32[2,3,128,128]{3,2,1,0:T(8,128)S(1)}, u32[]{:S(2)}, u32[]{:S(2)}) collective-permute-start(f32[2,3,128,128]{3,2,1,0:T(8,128)S(1)} %get-tuple-element.64.refs_3_), channel_id=1, source_target_pairs={{4,8},{8,4},{12,16},{16,12},{20,24},{24,20},{28,32},{32,28},{36,40... | collective-permute-start | bytes 1179656 | tf_op jit(solution)/shard_map/ppermute | solution.py:405
  110.8 11.6 %collective-permute-start.14 = (f32[2,3,128,128]{3,2,1,0:T(8,128)S(1)}, f32[2,3,128,128]{3,2,1,0:T(8,128)S(1)}, u32[]{:S(2)}, u32[]{:S(2)}) collective-permute-start(f32[2,3,128,128]{3,2,1,0:T(8,128)S(1)} %get-tuple-element.65), channel_id=1, source_target_pairs={{0,1},{1,0},{2,3},{3,2},{4,5},{5,4},{6,7},{7,6},{8,9},{9,8},{10,11... | collective-permute-start | bytes 1179656 | tf_op jit(solution)/shard_map/ppermute | solution.py:404
  111.5 10.9 %collective-permute-start.15 = (f32[2,3,128,128]{3,2,1,0:T(8,128)S(1)}, f32[2,3,128,128]{3,2,1,0:T(8,128)S(1)}, u32[]{:S(2)}, u32[]{:S(2)}) collective-permute-start(f32[2,3,128,128]{3,2,1,0:T(8,128)S(1)} %get-tuple-element.66), channel_id=1, source_target_pairs={{1,2},{2,1},{5,6},{6,5},{9,10},{10,9},{13,14},{14,13},{17,18},{18,... | collective-permute-start | bytes 1179656 | tf_op jit(solution)/shard_map/ppermute | solution.py:403
  122.9 8.8 %collective-permute-start.16 = (f32[2,3,128,128]{3,2,1,0:T(8,128)S(1)}, f32[2,3,128,128]{3,2,1,0:T(8,128)S(1)}, u32[]{:S(2)}, u32[]{:S(2)}) collective-permute-start(f32[2,3,128,128]{3,2,1,0:T(8,128)S(1)} %get-tuple-element.69.refs_2_), channel_id=1, source_target_pairs={{0,4},{4,0},{8,12},{12,8},{16,20},{20,16},{24,28},{28,24},{32,36},... | collective-permute-start | bytes 1179656 | tf_op jit(solution)/shard_map/ppermute | solution.py:406
  123.2 9.1 %collective-permute-start.17 = (f32[2,3,128,128]{3,2,1,0:T(8,128)S(1)}, f32[2,3,128,128]{3,2,1,0:T(8,128)S(1)}, u32[]{:S(2)}, u32[]{:S(2)}) collective-permute-start(f32[2,3,128,128]{3,2,1,0:T(8,128)S(1)} %get-tuple-element.70.refs_3_), channel_id=1, source_target_pairs={{4,8},{8,4},{12,16},{16,12},{20,24},{24,20},{28,32},{32,28},{36,40... | collective-permute-start | bytes 1179656 | tf_op jit(solution)/shard_map/ppermute | solution.py:405
  125.6 13.4 %collective-permute-start.18 = (f32[2,3,128,128]{3,2,1,0:T(8,128)S(1)}, f32[2,3,128,128]{3,2,1,0:T(8,128)S(1)}, u32[]{:S(2)}, u32[]{:S(2)}) collective-permute-start(f32[2,3,128,128]{3,2,1,0:T(8,128)S(1)} %get-tuple-element.71), channel_id=1, source_target_pairs={{0,1},{1,0},{2,3},{3,2},{4,5},{5,4},{6,7},{7,6},{8,9},{9,8},{10,11... | collective-permute-start | bytes 1179656 | tf_op jit(solution)/shard_map/ppermute | solution.py:404
  129.3 9.7 %collective-permute-start.19 = (f32[2,3,128,128]{3,2,1,0:T(8,128)S(1)}, f32[2,3,128,128]{3,2,1,0:T(8,128)S(1)}, u32[]{:S(2)}, u32[]{:S(2)}) collective-permute-start(f32[2,3,128,128]{3,2,1,0:T(8,128)S(1)} %get-tuple-element.72), channel_id=1, source_target_pairs={{1,2},{2,1},{5,6},{6,5},{9,10},{10,9},{13,14},{14,13},{17,18},{18,... | collective-permute-start | bytes 1179656 | tf_op jit(solution)/shard_map/ppermute | solution.py:403
  140.5 12.3 %collective-permute-start.20 = (f32[2,3,128,128]{3,2,1,0:T(8,128)}, f32[2,3,128,128]{3,2,1,0:T(8,128)S(1)}, u32[]{:S(2)}, u32[]{:S(2)}) collective-permute-start(f32[2,3,128,128]{3,2,1,0:T(8,128)} %get-tuple-element.73.refs_2_), channel_id=1, source_target_pairs={{0,4},{4,0},{8,12},{12,8},{16,20},{20,16},{24,28},{28,24},{32,36},... | collective-permute-start | bytes 1179656 | tf_op jit(solution)/shard_map/ppermute | solution.py:406
  140.7 12.2 %collective-permute-start.21 = (f32[2,3,128,128]{3,2,1,0:T(8,128)}, f32[2,3,128,128]{3,2,1,0:T(8,128)S(1)}, u32[]{:S(2)}, u32[]{:S(2)}) collective-permute-start(f32[2,3,128,128]{3,2,1,0:T(8,128)} %get-tuple-element.74.refs_3_), channel_id=1, source_target_pairs={{4,8},{8,4},{12,16},{16,12},{20,24},{24,20},{28,32},{32,28},{36,40... | collective-permute-start | bytes 1179656 | tf_op jit(solution)/shard_map/ppermute | solution.py:405
  143.6 13.8 %collective-permute-start.22 = (f32[2,3,128,128]{3,2,1,0:T(8,128)}, f32[2,3,128,128]{3,2,1,0:T(8,128)}, u32[]{:S(2)}, u32[]{:S(2)}) collective-permute-start(f32[2,3,128,128]{3,2,1,0:T(8,128)} %get-tuple-element.76), channel_id=1, source_target_pairs={{0,1},{1,0},{2,3},{3,2},{4,5},{5,4},{6,7},{7,6},{8,9},{9,8},{10,11... | collective-permute-start | bytes 1179656 | tf_op jit(solution)/shard_map/ppermute | solution.py:404
  147.7 9.6 %collective-permute-start.23 = (f32[2,3,128,128]{3,2,1,0:T(8,128)}, f32[2,3,128,128]{3,2,1,0:T(8,128)}, u32[]{:S(2)}, u32[]{:S(2)}) collective-permute-start(f32[2,3,128,128]{3,2,1,0:T(8,128)} %get-tuple-element.77), channel_id=1, source_target_pairs={{1,2},{2,1},{5,6},{6,5},{9,10},{10,9},{13,14},{14,13},{17,18},{18,... | collective-permute-start | bytes 1179656 | tf_op jit(solution)/shard_map/ppermute | solution.py:403
  (13 other events, 39.1 us)
